TPU v7x, 256 devices: a whole 4x4x8 slice. The times are simulated.
256 devices in a mesh: seq: 8 (over y_hi, x), row: 8 (over z), col: 4 (over y_lo, core).
Axes of the slice: x: 4, y: 4 (y_hi: 2, y_lo: 2; y = y_hi * 2 + y_lo), z: 8, core: 2. Of those that a mesh axis runs over, the one named last changes fastest.
Arguments:
- alignment: int32 [32768, 256], P('seq'), may hold values from 0 to 20, as said below
- cluster_sizes: int32 [32768], P('seq'), may hold values from 1 to 32, as said below
- block_inverse: float32 [128, 128], replicated, may hold values from -12 to 12
Outputs:
- couplings: float32 [5120, 5120], P(('seq', 'row'), 'col')
Inputs may be any that keep to these rules, and one draw needn't show every extreme that they name: `alignment`: the value 20 marks a gap. `cluster_sizes`: every cluster size is a power of two.
All inputs are finite; a program needn't handle non-finite values.
Results may differ from a plain program's by a relative error of at most 0.0003.
Values sent between devices are 32-bit elements; how exact they have to be, the bound alone decides.
A program may use at most 64 MiB of HBM per device.

v0:
```python
import jax
import jax.numpy as jnp
from jax import lax
from jax.sharding import PartitionSpec as P

Q = 20
POS = 256
PANEL = 128
PSEUDOCOUNT = 0.5


def spread(value, axis, source):
    kept = jnp.where(lax.axis_index(axis) == source, value, 0).astype(value.dtype)
    return lax.psum(kept, axis)


def one_hot_states(states):
    levels = lax.broadcasted_iota(jnp.int32, (1, 1, Q), 2)
    matches = (states[:, :, None] == levels).astype(jnp.bfloat16)
    return matches.reshape(states.shape[0], states.shape[1] * Q)


def covariance_block(pair_block, row_margin, col_margin, weight_total, row_start, col_start):
    row_freq = (1.0 - PSEUDOCOUNT) * row_margin / weight_total + PSEUDOCOUNT / Q
    col_freq = (1.0 - PSEUDOCOUNT) * col_margin / weight_total + PSEUDOCOUNT / Q
    shape_rc = pair_block.shape
    row_ids = row_start + lax.broadcasted_iota(jnp.int32, shape_rc, 0)
    col_ids = col_start + lax.broadcasted_iota(jnp.int32, shape_rc, 1)
    same_pos = row_ids // Q == col_ids // Q
    prior = jnp.where(
        same_pos, jnp.where(row_ids == col_ids, PSEUDOCOUNT / Q, 0.0), PSEUDOCOUNT / (Q * Q)
    )
    joint = (1.0 - PSEUDOCOUNT) * pair_block / weight_total + prior
    return joint - row_freq[:, None] * col_freq[None, :]


def accumulate_pairs(row_states, column_sets, span_widths, seq_weight):
    local_seqs = row_states.shape[0]
    block_rows = min(local_seqs, 1024)
    count_blocks = local_seqs // block_rows
    row_width = row_states.shape[1] * Q

    def blocked(states):
        return states.reshape(count_blocks, block_rows, states.shape[1])

    def add_block(running, block_item):
        pair_totals, row_margin, column_margins = running
        row_block, weight_block, column_blocks = block_item
        row_hot = one_hot_states(row_block)
        weighted = row_hot * weight_block[:, None]
        new_pairs = []
        new_margins = []
        for pair_total, margin_total, states_block, span_width in zip(
            pair_totals, column_margins, column_blocks, span_widths
        ):
            column_hot = one_hot_states(states_block)
            new_pairs.append(
                pair_total
                + lax.dot_general(
                    weighted,
                    column_hot,
                    (((0,), (0,)), ((), ())),
                    preferred_element_type=jnp.float32,
                )
            )
            new_margins.append(
                margin_total + jnp.dot(weight_block, column_hot, preferred_element_type=jnp.float32)
            )
        row_margin = row_margin + jnp.dot(weight_block, row_hot, preferred_element_type=jnp.float32)
        return ((tuple(new_pairs), row_margin, tuple(new_margins)), None)

    initial = (
        tuple((jnp.zeros((row_width, span_width), jnp.float32) for span_width in span_widths)),
        jnp.zeros((row_width,), jnp.float32),
        tuple((jnp.zeros((span_width,), jnp.float32) for span_width in span_widths)),
    )
    block_items = (
        blocked(row_states),
        seq_weight.reshape(count_blocks, block_rows),
        tuple((blocked(states) for states in column_sets)),
    )
    result, unused = lax.scan(add_block, initial, block_items)
    return result


def shards(alignment, cluster_sizes, block_inverse):
    seq_count = lax.axis_size("seq")
    row_count = lax.axis_size("row")
    col_count = lax.axis_size("col")
    seq_index = lax.axis_index("seq")
    row_index = lax.axis_index("row")
    col_index = lax.axis_index("col")
    local_seqs = alignment.shape[0]
    row_positions = POS // (seq_count * row_count)
    col_positions = POS // col_count
    block_features = row_positions * Q
    col_features = col_positions * Q
    seq_weight = (1.0 / cluster_sizes.astype(jnp.float32)).astype(jnp.bfloat16)
    grouped = alignment.reshape(local_seqs, seq_count, row_count, row_positions)
    row_states = lax.dynamic_slice_in_dim(grouped, row_index, 1, 2).reshape(
        local_seqs, seq_count * row_positions
    )
    col_states = lax.dynamic_slice_in_dim(alignment, col_index * col_positions, col_positions, 1)
    weight_local = jnp.sum(seq_weight.astype(jnp.float32))
    row_start = (seq_index * row_count + row_index) * block_features
    col_start = col_index * col_features
    pair_totals, row_margin, column_margins = accumulate_pairs(
        row_states, (col_states,), (col_features,), seq_weight
    )
    weight_total, row_margin, col_margin = lax.psum(
        (weight_local, row_margin, column_margins[0]), "seq"
    )
    pair_tile = lax.psum_scatter(pair_totals[0], "seq", scatter_dimension=0, tiled=True)
    own_margin = lax.dynamic_slice_in_dim(row_margin, seq_index * block_features, block_features)
    cov_tile = covariance_block(
        pair_tile, own_margin, col_margin, weight_total, row_start, col_start
    )
    panel_rows = spread(cov_tile[:, :PANEL], "col", 0)
    sym_inverse = 0.5 * (block_inverse + block_inverse.T)
    left_factor = jnp.dot(panel_rows, sym_inverse, precision=lax.Precision.HIGHEST)
    whole_panel = lax.all_gather(panel_rows, ("seq", "row"), axis=0, tiled=True)
    panel_cols = lax.dynamic_slice_in_dim(whole_panel, col_start, col_features, 0)
    update = lax.dot_general(
        left_factor, panel_cols, (((1,), (1,)), ((), ())), precision=lax.Precision.HIGHEST
    )
    return -Q * (cov_tile - update)


def solution(mesh):
    in_specs = (P("seq", None), P("seq"), P())
    out_specs = P(("seq", "row"), "col")
    return jax.shard_map(shards, mesh=mesh, in_specs=in_specs, out_specs=out_specs, check_vma=False)
```

profile of v0, /device:TPU:6, one launch (start us, length us, event | category | flops | bytes accessed | tf_op | source)
XLA Modules:
  0.0 306.2 jit_solution(9124577262664192869)
XLA Ops:
  6.5 5.6 %copy.9 = s32[4096,256]{0,1:T(8,128)} copy(s32[4096,256]{1,0:T(8,128)} %param.5) | data formatting | bytes 8388608 | tf_op args[0]
  12.1 2.2 constant_dynamic-slice_fusion.4
  14.3 0.6 copy.12
  14.9 5.2 %reshape.159 = s32[4096,8,8,4]{0,3,2,1:T(4,128)} reshape(s32[4096,256]{0,1:T(8,128)} %copy.9) | data formatting | bytes 8388608 | tf_op jit(solution)/shard_map/reshape | solution.py:99
  20.1 1.1 constant_dynamic-slice_fusion.5
  21.2 1.2 reshape_reshape.3
  22.5 0.7 convert_reduce_fusion
  23.1 51.7 %while.15 = (s32[]{:T(128)}, f32[640,1280]{1,0:T(8,128)}, f32[640]{0:T(1024)S(1)}, f32[1280]{0:T(1024)S(1)}, s32[4,1024,32]{1,0,2:T(4,128)}, /*index=5*/bf16[4,1...) while((s32[]{:T(128)}, f32[640,1280]{1,0:T(8,128)}, f32[640]{0:T(1024)S(1)}, ...), condition=%wide.region_1.2_spmd.clone, body=%wide.region_0.0_spmd.clone.sunk | while | flops 1686572800 | bytes 30978228 | solution.py:82
  23.2 1.5 constant_dynamic-slice_fusion.7
  24.8 0.5 broadcast_select_fusion.2
  25.2 1.2 mul.117
  26.5 0.9 iota_compare_fusion.4
  27.4 0.7 eq.120
  28.2 5.0 %convolution_add_fusion.2 = f32[640,1280]{1,0:T(8,128)} fusion(bf16[1024,640]{0,1:T(8,128)(2,1)} %mul.117, pred[1024,1280]{0,1:T(32,128)(4,1)S(1)} %eq.120, f32[640,1280]{1,0:T(8,128)} %get-tuple-element.161, pred[]{:T(512)S(6)} %compare.3), kind=kOutput, calls=%fused_computation.1.clone.1 | convolution fusion | flops 1679360000 | bytes 9175041 | tf_op jit(solution)/shard_map/while/body/eval_jaxpr/dot_general | solution.py:59
  33.2 0.8 convolution_reduce_fusion.5
  34.8 0.5 convolution_reduce_fusion.4
  35.4 1.5 constant_dynamic-slice_fusion.7
  36.9 0.5 broadcast_select_fusion.2
  37.4 1.2 mul.117
  38.7 0.9 iota_compare_fusion.4
  39.6 0.7 eq.120
  40.3 6.0 %convolution_add_fusion.2 = f32[640,1280]{1,0:T(8,128)} fusion(bf16[1024,640]{0,1:T(8,128)(2,1)} %mul.117, pred[1024,1280]{0,1:T(32,128)(4,1)S(1)} %eq.120, f32[640,1280]{1,0:T(8,128)} %get-tuple-element.161, pred[]{:T(512)S(6)} %compare.3), kind=kOutput, calls=%fused_computation.1.clone.1 | convolution fusion | flops 1679360000 | bytes 9175041 | tf_op jit(solution)/shard_map/while/body/eval_jaxpr/dot_general | solution.py:59
  46.4 0.8 convolution_reduce_fusion.5
  48.0 0.5 convolution_reduce_fusion.4
  48.5 1.5 constant_dynamic-slice_fusion.7
  50.1 0.5 broadcast_select_fusion.2
  50.6 1.2 mul.117
  51.8 0.9 iota_compare_fusion.4
  52.8 0.7 eq.120
  53.5 6.0 %convolution_add_fusion.2 = f32[640,1280]{1,0:T(8,128)} fusion(bf16[1024,640]{0,1:T(8,128)(2,1)} %mul.117, pred[1024,1280]{0,1:T(32,128)(4,1)S(1)} %eq.120, f32[640,1280]{1,0:T(8,128)} %get-tuple-element.161, pred[]{:T(512)S(6)} %compare.3), kind=kOutput, calls=%fused_computation.1.clone.1 | convolution fusion | flops 1679360000 | bytes 9175041 | tf_op jit(solution)/shard_map/while/body/eval_jaxpr/dot_general | solution.py:59
  59.6 0.8 convolution_reduce_fusion.5
  61.2 0.5 convolution_reduce_fusion.4
  61.7 1.5 constant_dynamic-slice_fusion.7
  63.3 0.5 broadcast_select_fusion.2
  63.8 1.2 mul.117
  65.0 0.9 iota_compare_fusion.4
  66.0 0.7 eq.120
  66.7 6.0 %convolution_add_fusion.2 = f32[640,1280]{1,0:T(8,128)} fusion(bf16[1024,640]{0,1:T(8,128)(2,1)} %mul.117, pred[1024,1280]{0,1:T(32,128)(4,1)S(1)} %eq.120, f32[640,1280]{1,0:T(8,128)} %get-tuple-element.161, pred[]{:T(512)S(6)} %compare.3), kind=kOutput, calls=%fused_computation.1.clone.1 | convolution fusion | flops 1679360000 | bytes 9175041 | tf_op jit(solution)/shard_map/while/body/eval_jaxpr/dot_general | solution.py:59
  72.8 0.8 convolution_reduce_fusion.5
  75.0 36.3 %all-reduce = (f32[1280]{0:T(1024)S(1)}, f32[]{:T(128)}, f32[640]{0:T(1024)S(1)}) all-reduce(f32[1280]{0:T(1024)S(1)} %get-tuple-element.46, f32[]{:T(128)} %get-tuple-element.102, f32[640]{0:T(1024)S(1)} %get-tuple-element.45), channel_id=1, replica_groups=mesh['seq'=8,'row'=8,'col'=4] {'seq'}, use_global_device_ids=true, to_apply=%region_6.7 | all-reduce | flops 1921 | bytes 15368 | tf_op jit(solution)/shard_map/psum | solution.py:110
  111.3 0.7 divide_add_fusion.1
  112.1 0.7 divide_add_fusion
  112.7 51.2 %reduce-scatter.2.cloned.1.call-done = f32[80,1280]{1,0:T(8,128)} async-done(((f32[640,1280]{1,0:T(8,128)}), f32[80,1280]{1,0:T(8,128)}) %reduce-scatter.2.cloned.1.call-update) | async-done | bytes 409616 | tf_op jit(solution)/shard_map/reduce_scatter | solution.py:113
  163.9 1.8 multiply_subtract_fusion
  165.8 11.4 %psum.31 = f32[80,128]{1,0:T(8,128)} all-reduce(f32[80,128]{1,0:T(8,128)S(1)} %slice_select_fusion), channel_id=1, replica_groups=mesh['seq'=8,'row'=8,'col'=4] {'col'}, use_global_device_ids=true, to_apply=%region_7.8 | all-reduce | flops 10240 | bytes 81920 | tf_op jit(solution)/shard_map/psum | solution.py:14
  177.3 1.0 fusion.6
  178.3 118.5 %all-gather.2.cloned.1.call-done = f32[5120,128]{1,0:T(8,128)} async-done(((f32[80,128]{1,0:T(8,128)}), f32[5120,128]{1,0:T(8,128)}) %all-gather.2.cloned.1.call-update) | async-done | bytes 2621456 | tf_op jit(solution)/shard_map/all_gather | solution.py:121
  296.8 2.6 fusion.3
  (65 shorter events, 4.2 us)
Async XLA Ops:
  6.5 157.4 %reduce-scatter.2.cloned.1.call-start = ((), (), s32[]{:S(2)}) async-start(), calls=%async_computation.1 | async-start | bytes 3686400 | tf_op jit(solution)/shard_map/reduce_scatter | solution.py:113
  20.1 2.3 copy-start.3
  23.1 3.3 %copy-start = (s32[4,1024,64]{1,2,0:T(8,128)}, s32[4,1024,64]{1,2,0:T(8,128)S(1)}, u32[]{:S(2)}) copy-start(s32[4,1024,64]{1,2,0:T(8,128)S(1)} %get-tuple-element.175) | copy-start | bytes 3145732 | tf_op jit(solution)/shard_map/while
  33.2 2.1 copy-start.1
  35.3 3.3 %copy-start = (s32[4,1024,64]{1,2,0:T(8,128)}, s32[4,1024,64]{1,2,0:T(8,128)S(1)}, u32[]{:S(2)}) copy-start(s32[4,1024,64]{1,2,0:T(8,128)S(1)} %get-tuple-element.175) | copy-start | bytes 3145732 | tf_op jit(solution)/shard_map/while
  46.4 2.1 copy-start.1
  48.5 3.3 %copy-start = (s32[4,1024,64]{1,2,0:T(8,128)}, s32[4,1024,64]{1,2,0:T(8,128)S(1)}, u32[]{:S(2)}) copy-start(s32[4,1024,64]{1,2,0:T(8,128)S(1)} %get-tuple-element.175) | copy-start | bytes 3145732 | tf_op jit(solution)/shard_map/while
  59.6 2.1 copy-start.1
  61.7 3.3 %copy-start = (s32[4,1024,64]{1,2,0:T(8,128)}, s32[4,1024,64]{1,2,0:T(8,128)S(1)}, u32[]{:S(2)}) copy-start(s32[4,1024,64]{1,2,0:T(8,128)S(1)} %get-tuple-element.175) | copy-start | bytes 3145732 | tf_op jit(solution)/shard_map/while
  72.8 2.1 copy-start.1
  74.9 102.3 %copy-start.2 = (f32[128,128]{1,0:T(8,128)S(1)}, f32[128,128]{1,0:T(8,128)}, u32[]{:S(2)}) copy-start(f32[128,128]{1,0:T(8,128)} %param.7) | copy-start | bytes 196612
  74.9 221.8 %all-gather.2.cloned.1.call-start = ((), (), s32[]{:S(2)}) async-start(), calls=%async_computation.2 | async-start | bytes 2662400 | tf_op jit(solution)/shard_map/all_gather | solution.py:121
Sparse Core Ops, SparseCore 0:
  75.0 88.8 reduce-scatter.1
  177.3 119.4 all-gather.1
where the time goes:
time: 307 us; the launch traced here: 306 us
  waiting for transfers between devices  170 us (55%)
  blocking collectives  47.6 us (16%)
  matrix products  31.8 us (10%)
  local copies, waits for them, and re-layouts  31.7 us (10%)
  between operations  13.5 us (4%)
  other arithmetic  11.4 us (4%)
    all_gather x1, waiting for transfers between devices, shards(): whole_panel = lax.all_gather(panel_rows, ('seq', 'row'), axis=0, tiled=True)  118 us
    reduce_scatter x1, waiting for transfers between devices, shards(): lax.psum_scatter(pair_totals[0], 'seq', scatter_dimension=0, tiled=True)  51.2 us
    psum x1, blocking collectives, shards(): lax.psum((weight_local, row_margin, column_margins[0]), 'seq')  36.3 us
    dot_general x4, matrix products, add_block(): lax.dot_general(weighted, column_hot, (((0,), (0,)), ((), ())), preferred...  23.1 us
    psum x1, blocking collectives, spread(): return lax.psum(kept, axis)  11.4 us
    dynamic_slice x12, local copies, waits for them, and re-layouts, accumulate_pairs(): result, unused = lax.scan(add_block, initial, block_items)  6.38 us
    unnamed x7, local copies, waits for them, and re-layouts  6.29 us
  transfers between devices with their start and end apart: 2, of which 2 were waited for; matrix products, arithmetic and copies ran while one was open for 1% of the time, Pallas kernels for 0%

commit v1 on v0

--- a/solution.py
+++ b/solution.py
@@ -9,9 +9,15 @@
 PSEUDOCOUNT = 0.5
 
 
+def add_all(shard, name):
+    parts = lax.all_gather(shard, name, axis=0, tiled=False)
+    total = parts.sum(axis=0)
+    return total
+
+
 def spread(value, axis, source):
     kept = jnp.where(lax.axis_index(axis) == source, value, 0).astype(value.dtype)
-    return lax.psum(kept, axis)
+    return add_all(kept, axis)
 
 
 def one_hot_states(states):

time: 307 us -> 302 us (0.984)
  blocking collectives: 47.6 us -> 41.8 us
    psum x1 -> x0, blocking collectives: 11.4 us -> none  [spread(): return lax.psum(kept, axis)]
    all_gather x0 -> x1, blocking collectives: none -> 5.52 us  [add_all(): parts = lax.all_gather(shard, name, axis=0, tiled=False)]
where the time goes in v1:
time: 302 us; the launch traced here: 301 us
  waiting for transfers between devices  170 us (56%)
  blocking collectives  41.8 us (14%)
  matrix products  31.8 us (11%)
  local copies, waits for them, and re-layouts  31.7 us (10%)
  between operations  13.5 us (4%)
  other arithmetic  12 us (4%)
    all_gather x1, waiting for transfers between devices, shards(): whole_panel = lax.all_gather(panel_rows, ('seq', 'row'), axis=0, tiled=True)  119 us
    reduce_scatter x1, waiting for transfers between devices, shards(): lax.psum_scatter(pair_totals[0], 'seq', scatter_dimension=0, tiled=True)  51.2 us
    psum x1, blocking collectives, shards(): lax.psum((weight_local, row_margin, column_margins[0]), 'seq')  36.3 us
    dot_general x4, matrix products, add_block(): lax.dot_general(weighted, column_hot, (((0,), (0,)), ((), ())), preferred...  23.1 us
    dynamic_slice x12, local copies, waits for them, and re-layouts, accumulate_pairs(): result, unused = lax.scan(add_block, initial, block_items)  6.38 us
    unnamed x7, local copies, waits for them, and re-layouts  6.29 us
  transfers between devices with their start and end apart: 2, of which 2 were waited for; matrix products, arithmetic and copies ran while one was open for 1% of the time, Pallas kernels for 0%

profile of v1, /device:TPU:6, one launch (start us, length us, event | category | flops | bytes accessed | tf_op | source)
XLA Modules:
  0.0 301.3 jit_solution(3417993990340295673)
XLA Ops:
  6.5 5.6 %copy.9 = s32[4096,256]{0,1:T(8,128)} copy(s32[4096,256]{1,0:T(8,128)} %param.5) | data formatting | bytes 8388608 | tf_op args[0]
  12.1 2.2 constant_dynamic-slice_fusion.4
  14.3 0.6 copy.12
  14.9 5.2 %reshape.159 = s32[4096,8,8,4]{0,3,2,1:T(4,128)} reshape(s32[4096,256]{0,1:T(8,128)} %copy.9) | data formatting | bytes 8388608 | tf_op jit(solution)/shard_map/reshape | solution.py:105
  20.1 1.1 constant_dynamic-slice_fusion.5
  21.2 1.2 reshape_reshape.3
  22.5 0.7 convert_reduce_fusion
  23.1 51.7 %while.15 = (s32[]{:T(128)}, f32[640,1280]{1,0:T(8,128)}, f32[640]{0:T(1024)S(1)}, f32[1280]{0:T(1024)S(1)}, s32[4,1024,32]{1,0,2:T(4,128)}, /*index=5*/bf16[4,1...) while((s32[]{:T(128)}, f32[640,1280]{1,0:T(8,128)}, f32[640]{0:T(1024)S(1)}, ...), condition=%wide.region_1.2_spmd.clone, body=%wide.region_0.0_spmd.clone.sunk | while | flops 1686572800 | bytes 30978228 | solution.py:88
  23.2 1.5 constant_dynamic-slice_fusion.7
  24.8 0.5 broadcast_select_fusion.2
  25.2 1.2 mul.117
  26.5 0.9 iota_compare_fusion.4
  27.4 0.7 eq.120
  28.2 5.0 %convolution_add_fusion.2 = f32[640,1280]{1,0:T(8,128)} fusion(bf16[1024,640]{0,1:T(8,128)(2,1)} %mul.117, pred[1024,1280]{0,1:T(32,128)(4,1)S(1)} %eq.120, f32[640,1280]{1,0:T(8,128)} %get-tuple-element.161, pred[]{:T(512)S(6)} %compare.3), kind=kOutput, calls=%fused_computation.1.clone.1 | convolution fusion | flops 1679360000 | bytes 9175041 | tf_op jit(solution)/shard_map/while/body/eval_jaxpr/dot_general | solution.py:65
  33.2 0.8 convolution_reduce_fusion.5
  34.8 0.5 convolution_reduce_fusion.4
  35.4 1.5 constant_dynamic-slice_fusion.7
  36.9 0.5 broadcast_select_fusion.2
  37.4 1.2 mul.117
  38.7 0.9 iota_compare_fusion.4
  39.6 0.7 eq.120
  40.3 6.0 %convolution_add_fusion.2 = f32[640,1280]{1,0:T(8,128)} fusion(bf16[1024,640]{0,1:T(8,128)(2,1)} %mul.117, pred[1024,1280]{0,1:T(32,128)(4,1)S(1)} %eq.120, f32[640,1280]{1,0:T(8,128)} %get-tuple-element.161, pred[]{:T(512)S(6)} %compare.3), kind=kOutput, calls=%fused_computation.1.clone.1 | convolution fusion | flops 1679360000 | bytes 9175041 | tf_op jit(solution)/shard_map/while/body/eval_jaxpr/dot_general | solution.py:65
  46.4 0.8 convolution_reduce_fusion.5
  48.0 0.5 convolution_reduce_fusion.4
  48.5 1.5 constant_dynamic-slice_fusion.7
  50.1 0.5 broadcast_select_fusion.2
  50.6 1.2 mul.117
  51.8 0.9 iota_compare_fusion.4
  52.8 0.7 eq.120
  53.5 6.0 %convolution_add_fusion.2 = f32[640,1280]{1,0:T(8,128)} fusion(bf16[1024,640]{0,1:T(8,128)(2,1)} %mul.117, pred[1024,1280]{0,1:T(32,128)(4,1)S(1)} %eq.120, f32[640,1280]{1,0:T(8,128)} %get-tuple-element.161, pred[]{:T(512)S(6)} %compare.3), kind=kOutput, calls=%fused_computation.1.clone.1 | convolution fusion | flops 1679360000 | bytes 9175041 | tf_op jit(solution)/shard_map/while/body/eval_jaxpr/dot_general | solution.py:65
  59.6 0.8 convolution_reduce_fusion.5
  61.7 1.5 constant_dynamic-slice_fusion.7
  63.3 0.5 broadcast_select_fusion.2
  63.8 1.2 mul.117
  65.0 0.9 iota_compare_fusion.4
  66.0 0.7 eq.120
  66.7 6.0 %convolution_add_fusion.2 = f32[640,1280]{1,0:T(8,128)} fusion(bf16[1024,640]{0,1:T(8,128)(2,1)} %mul.117, pred[1024,1280]{0,1:T(32,128)(4,1)S(1)} %eq.120, f32[640,1280]{1,0:T(8,128)} %get-tuple-element.161, pred[]{:T(512)S(6)} %compare.3), kind=kOutput, calls=%fused_computation.1.clone.1 | convolution fusion | flops 1679360000 | bytes 9175041 | tf_op jit(solution)/shard_map/while/body/eval_jaxpr/dot_general | solution.py:65
  72.8 0.8 convolution_reduce_fusion.5
  75.0 36.3 %all-reduce = (f32[1280]{0:T(1024)S(1)}, f32[]{:T(128)}, f32[640]{0:T(1024)S(1)}) all-reduce(f32[1280]{0:T(1024)S(1)} %get-tuple-element.46, f32[]{:T(128)} %get-tuple-element.102, f32[640]{0:T(1024)S(1)} %get-tuple-element.45), channel_id=1, replica_groups=mesh['seq'=8,'row'=8,'col'=4] {'seq'}, use_global_device_ids=true, to_apply=%region_6.7 | all-reduce | flops 1921 | bytes 15368 | tf_op jit(solution)/shard_map/psum | solution.py:116
  111.3 0.7 divide_add_fusion.1
  112.1 0.7 divide_add_fusion
  112.7 51.2 %reduce-scatter.2.cloned.1.call-done = f32[80,1280]{1,0:T(8,128)} async-done(((f32[640,1280]{1,0:T(8,128)}), f32[80,1280]{1,0:T(8,128)}) %reduce-scatter.2.cloned.1.call-update) | async-done | bytes 409616 | tf_op jit(solution)/shard_map/reduce_scatter | solution.py:119
  163.9 1.8 multiply_subtract_fusion
  165.8 5.5 %all-gather = f32[320,128]{1,0:T(8,128)S(1)} all-gather(f32[80,128]{1,0:T(8,128)S(1)} %slice_select_fusion), channel_id=2, replica_groups=mesh['seq'=8,'row'=8,'col'=4] {'col'}, dimensions={0}, use_global_device_ids=true | all-gather | bytes 204800 | tf_op jit(solution)/shard_map/all_gather | solution.py:13
  171.3 0.6 reduce_sum.19
  172.1 1.0 fusion.6
  173.0 118.7 %all-gather.3.cloned.1.call-done = f32[5120,128]{1,0:T(8,128)} async-done(((f32[80,128]{1,0:T(8,128)}), f32[5120,128]{1,0:T(8,128)}) %all-gather.3.cloned.1.call-update) | async-done | bytes 2621456 | tf_op jit(solution)/shard_map/all_gather | solution.py:127
  291.8 2.6 fusion.3
  (66 shorter events, 4.7 us)
Async XLA Ops:
  6.5 157.4 %reduce-scatter.2.cloned.1.call-start = ((), (), s32[]{:S(2)}) async-start(), calls=%async_computation.1 | async-start | bytes 3686400 | tf_op jit(solution)/shard_map/reduce_scatter | solution.py:119
  20.1 2.3 copy-start.3
  23.1 3.3 %copy-start = (s32[4,1024,64]{1,2,0:T(8,128)}, s32[4,1024,64]{1,2,0:T(8,128)S(1)}, u32[]{:S(2)}) copy-start(s32[4,1024,64]{1,2,0:T(8,128)S(1)} %get-tuple-element.175) | copy-start | bytes 3145732 | tf_op jit(solution)/shard_map/while
  33.2 2.1 copy-start.1
  35.3 3.3 %copy-start = (s32[4,1024,64]{1,2,0:T(8,128)}, s32[4,1024,64]{1,2,0:T(8,128)S(1)}, u32[]{:S(2)}) copy-start(s32[4,1024,64]{1,2,0:T(8,128)S(1)} %get-tuple-element.175) | copy-start | bytes 3145732 | tf_op jit(solution)/shard_map/while
  46.4 2.1 copy-start.1
  48.5 3.3 %copy-start = (s32[4,1024,64]{1,2,0:T(8,128)}, s32[4,1024,64]{1,2,0:T(8,128)S(1)}, u32[]{:S(2)}) copy-start(s32[4,1024,64]{1,2,0:T(8,128)S(1)} %get-tuple-element.175) | copy-start | bytes 3145732 | tf_op jit(solution)/shard_map/while
  59.6 2.1 copy-start.1
  61.7 3.3 %copy-start = (s32[4,1024,64]{1,2,0:T(8,128)}, s32[4,1024,64]{1,2,0:T(8,128)S(1)}, u32[]{:S(2)}) copy-start(s32[4,1024,64]{1,2,0:T(8,128)S(1)} %get-tuple-element.175) | copy-start | bytes 3145732 | tf_op jit(solution)/shard_map/while
  72.8 2.1 copy-start.1
  74.9 97.1 %copy-start.2 = (f32[128,128]{1,0:T(8,128)S(1)}, f32[128,128]{1,0:T(8,128)}, u32[]{:S(2)}) copy-start(f32[128,128]{1,0:T(8,128)} %param.7) | copy-start | bytes 196612
  74.9 216.9 %all-gather.3.cloned.1.call-start = ((), (), s32[]{:S(2)}) async-start(), calls=%async_computation.2 | async-start | bytes 2662400 | tf_op jit(solution)/shard_map/all_gather | solution.py:127
Sparse Core Ops, SparseCore 0:
  75.0 88.8 reduce-scatter.1
  172.1 119.6 all-gather.2
